TPU v7x, 128 devices: a whole 4x4x4 slice. The times are simulated.
128 devices in a mesh: space: 32 (over z, y, core), orb: 4 (over x).
Axes of the slice: x: 4, y: 4, z: 4, core: 2. Of those that a mesh axis runs over, the one named last changes fastest.
Arguments:
- orbitals: float32 [8, 32768, 256], P('orb', 'space'), may hold values from -6 to 6
- near_source: int32 [32768, 27], P('space'), may hold values from 0 to 32767, as said below
- far_leaf: int32 [32768, 108], P('space'), may hold values from 0 to 32767, as said below
- far_mid: int32 [4096, 108], P('space'), may hold values from 0 to 4095, as said below
- far_top: int32 [512, 108], P('space'), may hold values from 0 to 511, as said below
- leaf_basis: bfloat16 [64, 256], replicated, may hold values from -0.375 to 0.375
- near_table: bfloat16 [27, 256, 256], replicated, may hold values from -0.078125 to 0.078125
- transfer: bfloat16 [8, 64, 64], replicated, may hold values from -0.75 to 0.75
- coupling: bfloat16 [108, 64, 64], replicated, may hold values from -0.078125 to 0.078125
- pair_transfer: bfloat16 [2, 64, 64], replicated, may hold values from -0.75 to 0.75
- coarse_coupling: bfloat16 [4, 64, 64], replicated, may hold values from -0.4375 to 0.4375
Outputs:
- relaxed: float32 [8, 32768, 256], P('orb', 'space')
Inputs may be any that keep to these rules, and one draw needn't show every extreme that they name: `near_source`: with layer(t) = t // 64: every entry of leaf t lies in a layer at most 1 from layer(t); entry 13 is t itself; entry 0 is the leaf at t's transverse position one layer away. `far_leaf`: with layer(t) = t // 64: every entry of box t lies in a layer 2 or 3 away from layer(t); entry 0 is exactly 3 layers away. `far_mid`: with layer(t) = t // 16: every entry of box t lies in a layer 2 or 3 away from layer(t); entry 0 is exactly 3 layers away. `far_top`: with layer(t) = t // 4: every entry of box t lies in a layer 2 or 3 away from layer(t); entry 0 is exactly 3 layers away.
All inputs are finite; a program needn't handle non-finite values.
Results may differ from a plain program's by a relative error of at most 0.012.
Values may be sent and summed in bfloat16 or wider, within the bound.
A program may use at most 192 MiB of HBM per device.

v0:
```python
import jax
import jax.numpy as jnp
from jax import lax
from jax.sharding import PartitionSpec as P

SIDE = 8
relax_step = 0.1


def padded(cells, sides, width):
    for axis, dim in sides:
        count = lax.axis_size(axis)
        ends = count - 1
        head = lax.slice_in_dim(cells, 0, width, axis=dim)
        tail = lax.slice_in_dim(cells, cells.shape[dim] - width, cells.shape[dim], axis=dim)
        cells = jnp.concatenate(
            [
                lax.ppermute(tail, axis, [(i, (i + 1) % count) for i in range(ends)]),
                cells,
                lax.ppermute(head, axis, [((i + 1) % count, i) for i in range(ends)]),
            ],
            axis=dim,
        )
    return cells


def leaf_project(density, leaf_basis):
    return jnp.einsum(
        "olp,rp->lor", density, leaf_basis, preferred_element_type=jnp.float32
    ).astype(jnp.bfloat16)


def octant_up(moments, side_boxes, transfer):
    node_count, orbits, rank_width = moments.shape
    layers = node_count // (side_boxes * side_boxes)
    half_side = side_boxes // 2
    shaped = moments.reshape(layers // 2, 2, half_side, 2, half_side, 2, orbits, rank_width)
    octant_grid = transfer.reshape(2, 2, 2, rank_width, rank_width)
    parents = jnp.einsum(
        "apbqcuos,pqusr->abcor", shaped, octant_grid, preferred_element_type=jnp.float32
    )
    return parents.reshape(-1, orbits, rank_width).astype(jnp.bfloat16)


def octant_down(coeffs, side_boxes, transfer):
    node_count, orbits, rank_width = coeffs.shape
    layers = node_count // (side_boxes * side_boxes)
    shaped = coeffs.reshape(layers, side_boxes, side_boxes, orbits, rank_width)
    octant_grid = transfer.reshape(2, 2, 2, rank_width, rank_width)
    children = jnp.einsum(
        "abcor,pqusr->apbqcuos", shaped, octant_grid, preferred_element_type=jnp.float32
    )
    return children.reshape(-1, orbits, rank_width)


def couple_rows(moments, sources, coupling, scale):
    node_count, orbits, rank_width = moments.shape
    flattened = moments.reshape(node_count, orbits * rank_width)
    identity = jnp.eye(orbits, dtype=coupling.dtype)
    running = None
    for column_start in range(0, sources.shape[1], 27):
        block_coupling = coupling[column_start : column_start + 27]
        widened = jnp.einsum("ab,krs->kasbr", identity, block_coupling).reshape(
            block_coupling.shape[0], orbits * rank_width, orbits * rank_width
        )
        picked = jnp.take(flattened, sources[:, column_start : column_start + 27], axis=0)
        piece_sum = jnp.einsum("lkx,kxy->ly", picked, widened, preferred_element_type=jnp.float32)
        running = piece_sum if running is None else running + piece_sum
    return scale * running.reshape(-1, orbits, rank_width)


def near_sum(density, sources, near_table):
    running = None
    for column_start in range(0, sources.shape[1], 9):
        picked = jnp.take(density, sources[:, column_start : column_start + 9], axis=1)
        piece_sum = jnp.einsum(
            "olkq,kpq->olp",
            picked,
            near_table[column_start : column_start + 9],
            preferred_element_type=jnp.float32,
        )
        running = piece_sum if running is None else running + piece_sum
    return running


def shifted(values, offset):
    node_count = values.shape[0]
    if abs(offset) >= node_count:
        return jnp.zeros_like(values)
    empty = jnp.zeros((abs(offset), values.shape[1], values.shape[2]), values.dtype)
    if offset > 0:
        return jnp.concatenate([values[offset:], empty], axis=0)
    return jnp.concatenate([empty, values[:offset]], axis=0)


def coarse_couple(moments, coarse_coupling, scale):
    node_count = moments.shape[0]
    odd_rows = (jnp.arange(node_count) % 2).astype(jnp.float32)[:, None, None]
    even_rows = 1.0 - odd_rows

    def apply_matrix(which, offset):
        return jnp.einsum(
            "nos,rs->nor",
            shifted(moments, offset),
            coarse_coupling[which],
            preferred_element_type=jnp.float32,
        )

    running = (
        apply_matrix(1, -2)
        + apply_matrix(2, 2)
        + even_rows * apply_matrix(3, 3)
        + odd_rows * apply_matrix(0, -3)
    )
    return scale * running


def coarse_up(moments, pair_transfer):
    node_count, orbits, rank_width = moments.shape
    shaped = moments.reshape(-1, 2, orbits, rank_width)
    return jnp.einsum(
        "apos,psr->aor", shaped, pair_transfer, preferred_element_type=jnp.float32
    ).astype(jnp.bfloat16)


def coarse_down(coeffs, pair_transfer):
    children = jnp.einsum(
        "aor,psr->apos", coeffs, pair_transfer, preferred_element_type=jnp.float32
    )
    return children.reshape(-1, coeffs.shape[1], coeffs.shape[2])


def coarse_tree(cube_moments, coarse_coupling, pair_transfer):
    levels = [cube_moments]
    while levels[-1].shape[0] > 1:
        levels.append(coarse_up(levels[-1], pair_transfer))
    top_level = len(levels) - 1
    coeffs = coarse_couple(levels[top_level], coarse_coupling, 0.5 ** (3 + top_level)).astype(
        jnp.bfloat16
    )
    for depth_level in range(top_level - 1, -1, -1):
        pushed = coarse_down(coeffs, pair_transfer)
        coupled = coarse_couple(levels[depth_level], coarse_coupling, 0.5 ** (3 + depth_level))
        coeffs = (coupled + pushed).astype(jnp.bfloat16)
    return coeffs


def shards(
    orbitals,
    near_source,
    far_leaf,
    far_mid,
    far_top,
    leaf_basis,
    near_table,
    transfer,
    coupling,
    pair_transfer,
    coarse_coupling,
):
    orbits, leaf_count, points = orbitals.shape
    rank_size = leaf_basis.shape[0]
    device = lax.axis_index("space")
    density = (orbitals * orbitals).astype(jnp.bfloat16)
    layer_size = SIDE * SIDE
    reach_leaves = 12 * layer_size
    density_ext = padded(density, (("space", 1),), layer_size)
    near_start = device * leaf_count - layer_size
    local_moments = leaf_project(density, leaf_basis)
    flattened = local_moments.reshape(leaf_count, orbits * rank_size)
    leaf_ext = padded(flattened, (("space", 0),), reach_leaves).reshape(-1, orbits, rank_size)
    near_field = near_sum(density_ext, near_source - near_start, near_table)
    mid_ext = octant_up(leaf_ext, SIDE, transfer)
    top_ext = octant_up(mid_ext, SIDE // 2, transfer)
    top_count = leaf_count // 64
    mid_count = leaf_count // 8
    top_rim = reach_leaves // 64
    mid_rim = reach_leaves // 8
    top_local = top_ext[top_rim : top_rim + top_count]
    cube_local = octant_up(top_local, SIDE // 4, transfer)
    cube_rows = cube_local.shape[0]
    cube_all = lax.all_gather(
        cube_local.reshape(cube_rows, orbits * rank_size), "space", axis=0, tiled=True
    ).reshape(-1, orbits, rank_size)
    cube_coeffs = coarse_tree(cube_all, coarse_coupling, pair_transfer)
    cube_own = lax.dynamic_slice_in_dim(cube_coeffs, device * cube_rows, cube_rows, 0)
    top_coeffs = (
        couple_rows(top_ext, far_top - (device * top_count - top_rim), coupling, 0.25)
        + octant_down(cube_own, SIDE // 8, transfer)
    ).astype(jnp.bfloat16)
    mid_coeffs = (
        couple_rows(mid_ext, far_mid - (device * mid_count - mid_rim), coupling, 0.5)
        + octant_down(top_coeffs, SIDE // 4, transfer)
    ).astype(jnp.bfloat16)
    leaf_coeffs = (
        couple_rows(leaf_ext, far_leaf - (device * leaf_count - reach_leaves), coupling, 1.0)
        + octant_down(mid_coeffs, SIDE // 2, transfer)
    ).astype(jnp.bfloat16)
    far_field = jnp.einsum(
        "lor,rp->olp", leaf_coeffs, leaf_basis, preferred_element_type=jnp.float32
    )
    potential = near_field + far_field
    hartree = lax.psum(jnp.sum(potential, axis=0).astype(jnp.bfloat16), "orb").astype(jnp.float32)
    return orbitals - relax_step * (hartree[None] - potential) * orbitals


def solution(mesh):
    placed = (
        P("orb", "space", None),
        P("space", None),
        P("space", None),
        P("space", None),
        P("space", None),
        P(),
        P(),
        P(),
        P(),
        P(),
        P(),
    )
    return jax.shard_map(
        shards, mesh=mesh, in_specs=placed, out_specs=P("orb", "space", None), check_vma=False
    )
```

profile of v0, /device:TPU:0, one launch (start us, length us, event | category | flops | bytes accessed | tf_op | source)
XLA Modules:
  0.0 1078.0 jit_solution(17902328975907240493)
XLA Ops:
  15.3 4.8 collective-permute-start
  55.0 9.0 multiply_bitcast_fusion
  77.4 4.4 reshape.258
  105.5 7.3 copy.392
  112.7 71.8 %gather_fusion.2 = bf16[9216,2,256]{2,1,0:T(2,128)(2,1)} fusion(bf16[2,1152,256]{2,0,1:T(2,128)(2,1)S(1)} %copy.392, s32[9216]{0:T(1024)S(1)} %broadcast_clamp_fusion.4), kind=kCustom, calls=%fused_computation.5.clone | custom fusion | bytes 18911232 | tf_op jit(solution)/shard_map/jit(_take)/gather | solution.py:75
  184.6 71.8 %gather_fusion.1 = bf16[9216,2,256]{2,1,0:T(2,128)(2,1)} fusion(bf16[2,1152,256]{2,0,1:T(2,128)(2,1)S(1)} %copy.392, s32[9216]{0:T(1024)S(1)} %broadcast_clamp_fusion.5), kind=kCustom, calls=%fused_computation.4.clone | custom fusion | bytes 18911232 | tf_op jit(solution)/shard_map/jit(_take)/gather | solution.py:75
  256.4 71.8 %gather_fusion = bf16[9216,2,256]{2,1,0:T(2,128)(2,1)} fusion(bf16[2,1152,256]{2,0,1:T(2,128)(2,1)S(1)} %copy.392, s32[9216]{0:T(1024)S(1)} %broadcast_clamp_fusion.6), kind=kCustom, calls=%fused_computation.clone | custom fusion | bytes 18911232 | tf_op jit(solution)/shard_map/jit(_take)/gather | solution.py:75
  328.2 18.5 %fusion.2 = bf16[2,1024,9,256]{3,0,2,1:T(2,128)(2,1)S(1)} fusion(bf16[1024,9,2,256]{3,2,1,0:T(2,128)(2,1)} %bitcast.386, pred[1024,9]{1,0:T(8,128)(4,1)S(1)} %copy-done.18), kind=kLoop, calls=%fused_computation.20 | loop fusion | flops 4718592 | bytes 18883584 | tf_op jit(solution)/shard_map/jit(_take)/select_n | solution.py:75
  350.8 16.6 %fusion.1 = bf16[2,1024,9,256]{3,0,2,1:T(2,128)(2,1)S(1)} fusion(bf16[1024,9,2,256]{3,2,1,0:T(2,128)(2,1)S(1)} %bitcast.385, pred[1024,9]{1,0:T(8,128)(4,1)S(1)} %copy-done.19), kind=kLoop, calls=%fused_computation.19 | loop fusion | flops 4718592 | bytes 18883584 | tf_op jit(solution)/shard_map/jit(_take)/select_n | solution.py:75
  367.5 18.0 %fusion = bf16[2,1024,9,256]{3,0,2,1:T(2,128)(2,1)} fusion(bf16[1024,9,2,256]{3,2,1,0:T(2,128)(2,1)S(1)} %bitcast.382, pred[1024,9]{1,0:T(8,128)(4,1)S(1)} %copy-done.20), kind=kLoop, calls=%fused_computation.18 | loop fusion | flops 4718592 | bytes 18883584 | tf_op jit(solution)/shard_map/jit(_take)/select_n | solution.py:75
  395.6 28.1 %all-gather = bf16[32,2,128]{2,1,0:T(2,128)(2,1)S(1)} all-gather(bf16[1,2,128]{2,1,0:T(2,128)(2,1)S(1)} %reshape.425), channel_id=1, replica_groups=mesh['space'=32,'orb'=4] {'space'}, dimensions={0}, use_global_device_ids=true | all-gather | bytes 16896 | tf_op jit(solution)/shard_map/all_gather | solution.py:182
  449.5 8.2 gather_fusion.10
  463.2 7.1 gather_fusion.9
  475.8 7.1 gather_fusion.8
  488.4 7.1 gather_fusion.7
  504.7 96.4 %gather_fusion.3 = bf16[27648,128]{1,0:T(8,128)(2,1)} fusion(bf16[2560,128]{1,0:T(8,128)(2,1)S(1)} %pad_maximum_fusion.1, s32[27648]{0:T(1024)S(1)} %broadcast_clamp_fusion.3), kind=kCustom, calls=%fused_computation.1.clone | custom fusion | bytes 14266368 | tf_op jit(solution)/shard_map/jit(_take)/gather | solution.py:66
  601.1 11.9 %reshape.448 = bf16[1024,27,128]{2,1,0:T(8,128)(2,1)} reshape(bf16[27648,128]{1,0:T(8,128)(2,1)} %gather_fusion.3) | data formatting | bytes 14155776 | tf_op jit(solution)/shard_map/jit(_take)/gather | solution.py:66
  613.1 15.5 %broadcast_select_fusion.6 = bf16[1024,27,128]{2,1,0:T(8,128)(2,1)S(1)} fusion(bf16[1024,27,128]{2,1,0:T(8,128)(2,1)} %reshape.448, pred[1024,27]{1,0:T(8,128)(4,1)S(1)} %copy-done.17), kind=kLoop, calls=%fused_computation.30 | loop fusion | flops 3538944 | bytes 14183424 | tf_op jit(solution)/shard_map/jit(_take)/select_n | solution.py:66
  632.9 96.4 %gather_fusion.4 = bf16[27648,128]{1,0:T(8,128)(2,1)} fusion(bf16[2560,128]{1,0:T(8,128)(2,1)S(1)} %pad_maximum_fusion.1, s32[27648]{0:T(1024)S(1)} %broadcast_clamp_fusion.2), kind=kCustom, calls=%fused_computation.6.clone | custom fusion | bytes 14266368 | tf_op jit(solution)/shard_map/jit(_take)/gather | solution.py:66
  729.3 11.9 %reshape.452 = bf16[1024,27,128]{2,1,0:T(8,128)(2,1)} reshape(bf16[27648,128]{1,0:T(8,128)(2,1)} %gather_fusion.4) | data formatting | bytes 14155776 | tf_op jit(solution)/shard_map/jit(_take)/gather | solution.py:66
  741.2 96.4 %gather_fusion.5 = bf16[27648,128]{1,0:T(8,128)(2,1)} fusion(bf16[2560,128]{1,0:T(8,128)(2,1)S(1)} %pad_maximum_fusion.1, s32[27648]{0:T(1024)S(1)} %broadcast_clamp_fusion.1), kind=kCustom, calls=%fused_computation.7.clone | custom fusion | bytes 14266368 | tf_op jit(solution)/shard_map/jit(_take)/gather | solution.py:66
  837.6 11.9 %reshape.456 = bf16[1024,27,128]{2,1,0:T(8,128)(2,1)} reshape(bf16[27648,128]{1,0:T(8,128)(2,1)} %gather_fusion.5) | data formatting | bytes 14155776 | tf_op jit(solution)/shard_map/jit(_take)/gather | solution.py:66
  849.5 96.4 %gather_fusion.6 = bf16[27648,128]{1,0:T(8,128)(2,1)} fusion(bf16[2560,128]{1,0:T(8,128)(2,1)S(1)} %pad_maximum_fusion.1, s32[27648]{0:T(1024)S(1)} %copy-done.4), kind=kCustom, calls=%fused_computation.8.clone | custom fusion | bytes 14266368 | tf_op jit(solution)/shard_map/jit(_take)/gather | solution.py:66
  945.9 11.9 %reshape.460 = bf16[1024,27,128]{2,1,0:T(8,128)(2,1)} reshape(bf16[27648,128]{1,0:T(8,128)(2,1)} %gather_fusion.6) | data formatting | bytes 14155776 | tf_op jit(solution)/shard_map/jit(_take)/gather | solution.py:66
  957.9 15.4 %broadcast_select_fusion.5 = bf16[1024,27,128]{2,1,0:T(8,128)(2,1)S(1)} fusion(bf16[1024,27,128]{2,1,0:T(8,128)(2,1)} %reshape.452, pred[1024,27]{1,0:T(8,128)(4,1)S(1)} %copy-done.14), kind=kLoop, calls=%fused_computation.29 | loop fusion | flops 3538944 | bytes 14183424 | tf_op jit(solution)/shard_map/jit(_take)/select_n | solution.py:66
  973.3 4.3 fusion.37
  977.7 15.7 %broadcast_select_fusion.4 = bf16[1024,27,128]{2,1,0:T(8,128)(2,1)S(1)} fusion(bf16[1024,27,128]{2,1,0:T(8,128)(2,1)} %reshape.456, pred[1024,27]{1,0:T(8,128)(4,1)S(1)} %copy-done.15), kind=kLoop, calls=%fused_computation.28 | loop fusion | flops 3538944 | bytes 14183424 | tf_op jit(solution)/shard_map/jit(_take)/select_n | solution.py:66
  993.5 4.3 fusion.34
  997.8 13.7 %broadcast_select_fusion.3 = bf16[1024,27,128]{2,1,0:T(8,128)(2,1)S(1)} fusion(bf16[1024,27,128]{2,1,0:T(8,128)(2,1)S(1)} %bitcast.388, pred[1024,27]{1,0:T(8,128)(4,1)S(1)} %copy-done.16), kind=kLoop, calls=%fused_computation.27 | loop fusion | flops 3538944 | bytes 14183424 | tf_op jit(solution)/shard_map/jit(_take)/select_n | solution.py:66
  1011.6 4.3 fusion.31
  1016.5 7.0 fusion.300
  1023.5 43.0 %all-reduce.22.cloned.1.call-done = bf16[1024,256]{1,0:T(8,128)(2,1)} async-done(((bf16[1024,256]{1,0:T(8,128)(2,1)}), bf16[1024,256]{1,0:T(8,128)(2,1)}) %all-reduce.22.cloned.1.call-update) | async-done | bytes 524304 | tf_op jit(solution)/shard_map/psum | solution.py:203
  (335 shorter events, 154.4 us)
Async XLA Ops:
  6.5 387.6 %copy-start = (bf16[8,64,64]{2,1,0:T(8,128)(2,1)S(1)}, bf16[8,64,64]{2,1,0:T(8,128)(2,1)}, u32[]{:S(2)}) copy-start(bf16[8,64,64]{2,1,0:T(8,128)(2,1)} %param.26) | copy-start | bytes 196612
  6.5 29.9 %copy-start.11 = (bf16[4,64,64]{2,1,0:T(8,128)(2,1)S(1)}, bf16[4,64,64]{2,1,0:T(8,128)(2,1)}, u32[]{:S(2)}) copy-start(bf16[4,64,64]{2,1,0:T(8,128)(2,1)} %param.29) | copy-start | bytes 98308
  6.5 25.2 %copy-start.24 = (s32[1024,108]{0,1:T(8,128)S(1)}, s32[1024,108]{0,1:T(8,128)}, u32[]{:S(2)}) copy-start(s32[1024,108]{0,1:T(8,128)} %param.21) | copy-start | bytes 1327108
  6.5 30.7 %copy-start.9 = (bf16[2,64,64]{2,1,0:T(8,128)(2,1)S(1)}, bf16[2,64,64]{2,1,0:T(8,128)(2,1)}, u32[]{:S(2)}) copy-start(bf16[2,64,64]{2,1,0:T(8,128)(2,1)} %param.28) | copy-start | bytes 49156
  6.5 34.3 %copy-start.2 = (bf16[108,64,64]{0,2,1:T(8,128)(2,1)S(1)}, bf16[108,64,64]{0,2,1:T(8,128)(2,1)}, u32[]{:S(2)}) copy-start(bf16[108,64,64]{0,2,1:T(8,128)(2,1)} %param.27) | copy-start | bytes 2654212
  6.5 1059.9 %all-reduce.22.cloned.1.call-start = ((), (), s32[]{:S(2)}) async-start(), calls=%async_computation | async-start | bytes 1048576 | tf_op jit(solution)/shard_map/psum | solution.py:203
  10.5 379.0 %collective-permute-start.2 = (bf16[768,128]{1,0:T(8,128)(2,1)}, bf16[768,128]{1,0:T(8,128)(2,1)}, u32[]{:S(2)}, u32[]{:S(2)}) collective-permute-start(bf16[768,128]{1,0:T(8,128)(2,1)} %copy.403), channel_id=1, source_target_pairs={{0,4},{4,8},{8,12},{12,16},{16,20},{20,24},{24,28},{28,32},{32,36}... | collective-permute-start | bytes 589832 | tf_op jit(solution)/shard_map/ppermute | solution.py:18
  13.3 376.3 %collective-permute-start.3 = (bf16[768,128]{1,0:T(8,128)(2,1)}, bf16[768,128]{1,0:T(8,128)(2,1)}, u32[]{:S(2)}, u32[]{:S(2)}) collective-permute-start(bf16[768,128]{1,0:T(8,128)(2,1)} %copy.404), channel_id=1, source_target_pairs={{4,0},{8,4},{12,8},{16,12},{20,16},{24,20},{28,24},{32,28},{36,32}... | collective-permute-start | bytes 589832 | tf_op jit(solution)/shard_map/ppermute | solution.py:20
  15.3 89.3 %collective-permute-start = (bf16[2,64,256]{2,1,0:T(8,128)(2,1)}, bf16[2,64,256]{2,1,0:T(8,128)(2,1)}, u32[]{:S(2)}, u32[]{:S(2)}) collective-permute-start(bf16[2,64,256]{2,1,0:T(8,128)(2,1)} %get-tuple-element.6), channel_id=1, source_target_pairs={{0,4},{4,8},{8,12},{12,16},{16,20},{20,24},{24,28},{28,32},{32,36}... | collective-permute-start | bytes 196616 | tf_op jit(solution)/shard_map/ppermute | solution.py:18
  20.1 84.4 %collective-permute-start.1 = (bf16[2,64,256]{2,1,0:T(8,128)(2,1)}, bf16[2,64,256]{2,1,0:T(8,128)(2,1)}, u32[]{:S(2)}, u32[]{:S(2)}) collective-permute-start(bf16[2,64,256]{2,1,0:T(8,128)(2,1)} %get-tuple-element.8), channel_id=1, source_target_pairs={{4,0},{8,4},{12,8},{16,12},{20,16},{24,20},{28,24},{32,28},{36,32}... | collective-permute-start | bytes 196616 | tf_op jit(solution)/shard_map/ppermute | solution.py:20
  64.0 19.5 %copy-start.35 = (s32[128,27]{0,1:T(8,128)S(1)}, s32[128,27]{0,1:T(8,128)}, u32[]{:S(2)}) copy-start(s32[128,27]{0,1:T(8,128)} %get-tuple-element.37) | copy-start | bytes 41476
  64.0 20.4 %copy-start.41 = (pred[128,27]{0,1:T(8,128)(4,1)S(1)}, pred[128,27]{0,1:T(8,128)(4,1)}, u32[]{:S(2)}) copy-start(pred[128,27]{0,1:T(8,128)(4,1)} %get-tuple-element.33) | copy-start | bytes 10372
  64.0 25.9 %copy-start.23 = (s32[1024,27]{0,1:T(8,128)S(1)}, s32[1024,27]{0,1:T(8,128)}, u32[]{:S(2)}) copy-start(s32[1024,27]{0,1:T(8,128)} %get-tuple-element.21) | copy-start | bytes 331780
  64.0 27.3 %copy-start.22 = (s32[1024,27]{0,1:T(8,128)S(1)}, s32[1024,27]{0,1:T(8,128)}, u32[]{:S(2)}) copy-start(s32[1024,27]{0,1:T(8,128)} %get-tuple-element.20) | copy-start | bytes 331780
  67.5 26.1 %copy-start.21 = (s32[1024,27]{0,1:T(8,128)S(1)}, s32[1024,27]{0,1:T(8,128)}, u32[]{:S(2)}) copy-start(s32[1024,27]{0,1:T(8,128)} %get-tuple-element.19) | copy-start | bytes 331780
  73.2 26.3 %copy-start.29 = (s32[1024,9]{0,1:T(8,128)S(1)}, s32[1024,9]{0,1:T(8,128)}, u32[]{:S(2)}) copy-start(s32[1024,9]{0,1:T(8,128)} %get-tuple-element.30) | copy-start | bytes 110596
  77.4 24.3 %copy-start.28 = (s32[1024,9]{0,1:T(8,128)S(1)}, s32[1024,9]{0,1:T(8,128)}, u32[]{:S(2)}) copy-start(s32[1024,9]{0,1:T(8,128)} %get-tuple-element.28) | copy-start | bytes 110596
  256.4 71.8 %copy-start.18 = (pred[1024,9]{1,0:T(8,128)(4,1)S(1)}, pred[1024,9]{1,0:T(8,128)(4,1)}, u32[]{:S(2)}) copy-start(pred[1024,9]{1,0:T(8,128)(4,1)} %copy.398) | copy-start | bytes 27652
  328.2 22.5 %slice-start.3 = ((s8[9437184]{0:T(1024)(128)(4,1)}), s8[4194304]{0:T(1024)(128)(4,1)S(1)}, s32[]{:S(2)}) async-start(s8[9437184]{0:T(1024)(128)(4,1)} %bitcast.383), calls=%async_computation.4 | async-start | bytes 8388608
  328.2 22.5 %slice-start.4 = ((s8[9437184]{0:T(1024)(128)(4,1)}), s8[4194304]{0:T(1024)(128)(4,1)S(1)}, s32[]{:S(2)}) async-start(s8[9437184]{0:T(1024)(128)(4,1)} %bitcast.383), calls=%async_computation.5 | async-start | bytes 8388608
  346.7 20.7 %slice-start = ((s8[9437184]{0:T(1024)(128)(4,1)}), s8[4194304]{0:T(1024)(128)(4,1)S(1)}, s32[]{:S(2)}) async-start(s8[9437184]{0:T(1024)(128)(4,1)} %bitcast.380), calls=%async_computation.1 | async-start | bytes 8388608
  346.7 20.7 %slice-start.1 = ((s8[9437184]{0:T(1024)(128)(4,1)}), s8[1048576]{0:T(1024)(128)(4,1)S(1)}, s32[]{:S(2)}) async-start(s8[9437184]{0:T(1024)(128)(4,1)} %bitcast.380), calls=%async_computation.2 | async-start | bytes 2097152
  389.5 34.2 %copy-start.10 = (bf16[2,64,64]{2,1,0:T(8,128)(2,1)S(1)}, bf16[2,64,64]{2,1,0:T(8,128)(2,1)}, u32[]{:S(2)}) copy-start(bf16[2,64,64]{2,1,0:T(8,128)(2,1)} %param.28) | copy-start | bytes 49156
  389.5 35.2 %copy-start.12 = (bf16[4,64,64]{2,1,0:T(8,128)(2,1)S(1)}, bf16[4,64,64]{2,1,0:T(8,128)(2,1)}, u32[]{:S(2)}) copy-start(bf16[4,64,64]{2,1,0:T(8,128)(2,1)} %param.29) | copy-start | bytes 98308
  389.5 47.4 %copy-start.37 = (s32[1024]{0:T(1024)S(1)}, s32[1024]{0:T(1024)}, u32[]{:S(2)}) copy-start(s32[1024]{0:T(1024)} %pad_clamp_fusion.7) | copy-start | bytes 12292
  389.5 49.0 %copy-start.38 = (s32[1024]{0:T(1024)S(1)}, s32[1024]{0:T(1024)}, u32[]{:S(2)}) copy-start(s32[1024]{0:T(1024)} %pad_clamp_fusion.6) | copy-start | bytes 12292
  389.6 51.2 %copy-start.39 = (s32[1024]{0:T(1024)S(1)}, s32[1024]{0:T(1024)}, u32[]{:S(2)}) copy-start(s32[1024]{0:T(1024)} %pad_clamp_fusion.5) | copy-start | bytes 12292
  394.7 54.3 %copy-start.6 = (bf16[27,128,128]{2,1,0:T(8,128)(2,1)S(1)}, bf16[27,128,128]{2,1,0:T(8,128)(2,1)}, u32[]{:S(2)}) copy-start(bf16[27,128,128]{2,1,0:T(8,128)(2,1)} %reshape.258) | copy-start | bytes 2654212
  973.3 24.5 %slice-start.6 = ((s8[8388608]{0:T(1024)(128)(4,1)}), s8[4194304]{0:T(1024)(128)(4,1)S(1)}, s32[]{:S(2)}) async-start(s8[8388608]{0:T(1024)(128)(4,1)} %bitcast.387), calls=%async_computation.7 | async-start | bytes 8388608
  977.7 20.1 %slice-start.7 = ((s8[8388608]{0:T(1024)(128)(4,1)}), s8[4194304]{0:T(1024)(128)(4,1)S(1)}, s32[]{:S(2)}) async-start(s8[8388608]{0:T(1024)(128)(4,1)} %bitcast.387), calls=%async_computation.8 | async-start | bytes 8388608
  1016.5 51.1 %copy-start.3 = (f32[2,1024,256]{2,1,0:T(8,128)S(1)}, f32[2,1024,256]{2,1,0:T(8,128)}, u32[]{:S(2)}) copy-start(f32[2,1024,256]{2,1,0:T(8,128)} %param.19) | copy-start | bytes 6291460
  1016.5 54.3 %copy-start.1 = (bf16[8,64,64]{2,1,0:T(8,128)(2,1)S(1)}, bf16[8,64,64]{2,1,0:T(8,128)(2,1)}, u32[]{:S(2)}) copy-start(bf16[8,64,64]{2,1,0:T(8,128)(2,1)} %param.26) | copy-start | bytes 196612
  (31 other events, 372.2 us)
Sparse Core Ops, SparseCore 0:
  1023.6 42.8 all-reduce.21
where the time goes:
time: 1090 us; the launch traced here: 1080 us
  local copies, waits for them, and re-layouts  761 us (70%)
  other arithmetic  162 us (15%)
  matrix products  58.8 us (5%)
  waiting for transfers between devices  43 us (4%)
  blocking collectives  28.1 us (3%)
  between operations  15 us (1%)
    gather x24, local copies, waits for them, and re-layouts, couple_rows(): jnp.take(flattened, sources[:, column_start:column_start + 27], axis=0)  475 us
    gather x3, local copies, waits for them, and re-layouts, near_sum(): jnp.take(density, sources[:, column_start:column_start + 9], axis=1)  215 us
    select_n x13, other arithmetic, couple_rows(): jnp.take(flattened, sources[:, column_start:column_start + 27], axis=0)  74.5 us
    select_n x4, other arithmetic, near_sum(): jnp.take(density, sources[:, column_start:column_start + 9], axis=1)  53.8 us
    psum x1, waiting for transfers between devices, shards(): lax.psum(jnp.sum(potential, axis=0).astype(jnp.bfloat16), 'orb')  43 us
    all_gather x1, blocking collectives, shards(): lax.all_gather(cube_local.reshape(cube_rows, orbits * rank_size), 'space'...  28.1 us
    dot_general x12, matrix products, couple_rows(): jnp.einsum('lkx,kxy->ly', picked, widened, preferred_element_type=jnp.flo...  26 us
  transfers between devices with their start and end apart: 5, of which 1 were waited for; matrix products, arithmetic and copies ran while one was open for 34% of the time, Pallas kernels for 0%

commit v1 on v0

--- a/solution.py
+++ b/solution.py
@@ -158,6 +158,11 @@
     pair_transfer,
     coarse_coupling,
 ):
+
+    def serve_columns(target, shard_axis):
+        piece_out = lax.all_gather(target, axis_name=shard_axis)
+        return jnp.sum(piece_out, 0)
+
     orbits, leaf_count, points = orbitals.shape
     rank_size = leaf_basis.shape[0]
     device = lax.axis_index("space")
@@ -200,7 +205,9 @@
         "lor,rp->olp", leaf_coeffs, leaf_basis, preferred_element_type=jnp.float32
     )
     potential = near_field + far_field
-    hartree = lax.psum(jnp.sum(potential, axis=0).astype(jnp.bfloat16), "orb").astype(jnp.float32)
+    hartree = serve_columns(jnp.sum(potential, axis=0).astype(jnp.bfloat16), "orb").astype(
+        jnp.float32
+    )
     return orbitals - relax_step * (hartree[None] - potential) * orbitals
 
 

time: 1090 us -> 1080 us (level)
  waiting for transfers between devices: 43 us -> 30.9 us
    psum x1 -> x0, waiting for transfers between devices: 43 us -> none  [shards(): lax.psum(jnp.sum(potential, axis=0).astype(jnp.bfloat16), 'orb')]
    all_gather x0 -> x1, waiting for transfers between devices: none -> 30.8 us  [serve_columns(): piece_out = lax.all_gather(target, axis_name=shard_axis)]
  transfers between devices with their start and end apart: 5 -> 5, of which waited for: 1 -> 1; matrix products, arithmetic and copies ran while one was open for 34% -> 35% of each run, Pallas kernels for 0% -> 0%
where the time goes in v1:
time: 1080 us; the launch traced here: 1070 us
  local copies, waits for them, and re-layouts  761 us (70%)
  other arithmetic  164 us (15%)
  matrix products  58.8 us (5%)
  waiting for transfers between devices  30.9 us (3%)
  blocking collectives  28.1 us (3%)
  between operations  15 us (1%)
    gather x24, local copies, waits for them, and re-layouts, couple_rows(): jnp.take(flattened, sources[:, column_start:column_start + 27], axis=0)  475 us
    gather x3, local copies, waits for them, and re-layouts, near_sum(): jnp.take(density, sources[:, column_start:column_start + 9], axis=1)  215 us
    select_n x13, other arithmetic, couple_rows(): jnp.take(flattened, sources[:, column_start:column_start + 27], axis=0)  74.5 us
    select_n x4, other arithmetic, near_sum(): jnp.take(density, sources[:, column_start:column_start + 9], axis=1)  53.8 us
    all_gather x1, waiting for transfers between devices, serve_columns(): piece_out = lax.all_gather(target, axis_name=shard_axis)  30.8 us
    all_gather x1, blocking collectives, shards(): lax.all_gather(cube_local.reshape(cube_rows, orbits * rank_size), 'space'...  28.1 us
    dot_general x12, matrix products, couple_rows(): jnp.einsum('lkx,kxy->ly', picked, widened, preferred_element_type=jnp.flo...  26 us
  transfers between devices with their start and end apart: 5, of which 1 were waited for; matrix products, arithmetic and copies ran while one was open for 35% of the time, Pallas kernels for 0%

profile of v1, /device:TPU:0, one launch (start us, length us, event | category | flops | bytes accessed | tf_op | source)
XLA Modules:
  0.0 1067.0 jit_solution(1161571349483743047)
XLA Ops:
  15.3 4.8 collective-permute-start
  55.0 9.0 multiply_bitcast_fusion
  77.4 4.4 reshape.268
  105.5 7.3 copy.476
  112.7 71.8 %gather_fusion.2 = bf16[9216,2,256]{2,1,0:T(2,128)(2,1)} fusion(bf16[2,1152,256]{2,0,1:T(2,128)(2,1)S(1)} %copy.476, s32[9216]{0:T(1024)S(1)} %broadcast_clamp_fusion.4), kind=kCustom, calls=%fused_computation.5.clone | custom fusion | bytes 18911232 | tf_op jit(solution)/shard_map/jit(_take)/gather | solution.py:75
  184.6 71.8 %gather_fusion.1 = bf16[9216,2,256]{2,1,0:T(2,128)(2,1)} fusion(bf16[2,1152,256]{2,0,1:T(2,128)(2,1)S(1)} %copy.476, s32[9216]{0:T(1024)S(1)} %broadcast_clamp_fusion.5), kind=kCustom, calls=%fused_computation.4.clone | custom fusion | bytes 18911232 | tf_op jit(solution)/shard_map/jit(_take)/gather | solution.py:75
  256.4 71.8 %gather_fusion = bf16[9216,2,256]{2,1,0:T(2,128)(2,1)} fusion(bf16[2,1152,256]{2,0,1:T(2,128)(2,1)S(1)} %copy.476, s32[9216]{0:T(1024)S(1)} %broadcast_clamp_fusion.6), kind=kCustom, calls=%fused_computation.clone | custom fusion | bytes 18911232 | tf_op jit(solution)/shard_map/jit(_take)/gather | solution.py:75
  328.2 18.5 %fusion.2 = bf16[2,1024,9,256]{3,0,2,1:T(2,128)(2,1)S(1)} fusion(bf16[1024,9,2,256]{3,2,1,0:T(2,128)(2,1)} %bitcast.387, pred[1024,9]{1,0:T(8,128)(4,1)S(1)} %copy-done.18), kind=kLoop, calls=%fused_computation.20 | loop fusion | flops 4718592 | bytes 18883584 | tf_op jit(solution)/shard_map/jit(_take)/select_n | solution.py:75
  350.8 16.6 %fusion.1 = bf16[2,1024,9,256]{3,0,2,1:T(2,128)(2,1)S(1)} fusion(bf16[1024,9,2,256]{3,2,1,0:T(2,128)(2,1)S(1)} %bitcast.386, pred[1024,9]{1,0:T(8,128)(4,1)S(1)} %copy-done.19), kind=kLoop, calls=%fused_computation.19 | loop fusion | flops 4718592 | bytes 18883584 | tf_op jit(solution)/shard_map/jit(_take)/select_n | solution.py:75
  367.5 18.0 %fusion = bf16[2,1024,9,256]{3,0,2,1:T(2,128)(2,1)} fusion(bf16[1024,9,2,256]{3,2,1,0:T(2,128)(2,1)S(1)} %bitcast.383, pred[1024,9]{1,0:T(8,128)(4,1)S(1)} %copy-done.20), kind=kLoop, calls=%fused_computation.18 | loop fusion | flops 4718592 | bytes 18883584 | tf_op jit(solution)/shard_map/jit(_take)/select_n | solution.py:75
  395.6 28.1 %all-gather.1 = bf16[32,2,128]{2,1,0:T(2,128)(2,1)S(1)} all-gather(bf16[1,2,128]{2,1,0:T(2,128)(2,1)S(1)} %reshape.436), channel_id=1, replica_groups=mesh['space'=32,'orb'=4] {'space'}, dimensions={0}, use_global_device_ids=true | all-gather | bytes 16896 | tf_op jit(solution)/shard_map/all_gather | solution.py:187
  449.5 8.2 gather_fusion.10
  463.2 7.1 gather_fusion.9
  475.8 7.1 gather_fusion.8
  488.4 7.1 gather_fusion.7
  504.7 96.4 %gather_fusion.3 = bf16[27648,128]{1,0:T(8,128)(2,1)} fusion(bf16[2560,128]{1,0:T(8,128)(2,1)S(1)} %pad_maximum_fusion.1, s32[27648]{0:T(1024)S(1)} %broadcast_clamp_fusion.3), kind=kCustom, calls=%fused_computation.1.clone | custom fusion | bytes 14266368 | tf_op jit(solution)/shard_map/jit(_take)/gather | solution.py:66
  601.1 11.9 %reshape.459 = bf16[1024,27,128]{2,1,0:T(8,128)(2,1)} reshape(bf16[27648,128]{1,0:T(8,128)(2,1)} %gather_fusion.3) | data formatting | bytes 14155776 | tf_op jit(solution)/shard_map/jit(_take)/gather | solution.py:66
  613.1 15.5 %broadcast_select_fusion.6 = bf16[1024,27,128]{2,1,0:T(8,128)(2,1)S(1)} fusion(bf16[1024,27,128]{2,1,0:T(8,128)(2,1)} %reshape.459, pred[1024,27]{1,0:T(8,128)(4,1)S(1)} %copy-done.17), kind=kLoop, calls=%fused_computation.30 | loop fusion | flops 3538944 | bytes 14183424 | tf_op jit(solution)/shard_map/jit(_take)/select_n | solution.py:66
  632.9 96.4 %gather_fusion.4 = bf16[27648,128]{1,0:T(8,128)(2,1)} fusion(bf16[2560,128]{1,0:T(8,128)(2,1)S(1)} %pad_maximum_fusion.1, s32[27648]{0:T(1024)S(1)} %broadcast_clamp_fusion.2), kind=kCustom, calls=%fused_computation.6.clone | custom fusion | bytes 14266368 | tf_op jit(solution)/shard_map/jit(_take)/gather | solution.py:66
  729.3 11.9 %reshape.463 = bf16[1024,27,128]{2,1,0:T(8,128)(2,1)} reshape(bf16[27648,128]{1,0:T(8,128)(2,1)} %gather_fusion.4) | data formatting | bytes 14155776 | tf_op jit(solution)/shard_map/jit(_take)/gather | solution.py:66
  741.2 96.4 %gather_fusion.5 = bf16[27648,128]{1,0:T(8,128)(2,1)} fusion(bf16[2560,128]{1,0:T(8,128)(2,1)S(1)} %pad_maximum_fusion.1, s32[27648]{0:T(1024)S(1)} %broadcast_clamp_fusion.1), kind=kCustom, calls=%fused_computation.7.clone | custom fusion | bytes 14266368 | tf_op jit(solution)/shard_map/jit(_take)/gather | solution.py:66
  837.6 11.9 %reshape.467 = bf16[1024,27,128]{2,1,0:T(8,128)(2,1)} reshape(bf16[27648,128]{1,0:T(8,128)(2,1)} %gather_fusion.5) | data formatting | bytes 14155776 | tf_op jit(solution)/shard_map/jit(_take)/gather | solution.py:66
  849.5 96.4 %gather_fusion.6 = bf16[27648,128]{1,0:T(8,128)(2,1)} fusion(bf16[2560,128]{1,0:T(8,128)(2,1)S(1)} %pad_maximum_fusion.1, s32[27648]{0:T(1024)S(1)} %copy-done.4), kind=kCustom, calls=%fused_computation.8.clone | custom fusion | bytes 14266368 | tf_op jit(solution)/shard_map/jit(_take)/gather | solution.py:66
  945.9 11.9 %reshape.471 = bf16[1024,27,128]{2,1,0:T(8,128)(2,1)} reshape(bf16[27648,128]{1,0:T(8,128)(2,1)} %gather_fusion.6) | data formatting | bytes 14155776 | tf_op jit(solution)/shard_map/jit(_take)/gather | solution.py:66
  957.9 15.4 %broadcast_select_fusion.5 = bf16[1024,27,128]{2,1,0:T(8,128)(2,1)S(1)} fusion(bf16[1024,27,128]{2,1,0:T(8,128)(2,1)} %reshape.463, pred[1024,27]{1,0:T(8,128)(4,1)S(1)} %copy-done.14), kind=kLoop, calls=%fused_computation.29 | loop fusion | flops 3538944 | bytes 14183424 | tf_op jit(solution)/shard_map/jit(_take)/select_n | solution.py:66
  973.3 4.3 fusion.37
  977.7 15.7 %broadcast_select_fusion.4 = bf16[1024,27,128]{2,1,0:T(8,128)(2,1)S(1)} fusion(bf16[1024,27,128]{2,1,0:T(8,128)(2,1)} %reshape.467, pred[1024,27]{1,0:T(8,128)(4,1)S(1)} %copy-done.15), kind=kLoop, calls=%fused_computation.28 | loop fusion | flops 3538944 | bytes 14183424 | tf_op jit(solution)/shard_map/jit(_take)/select_n | solution.py:66
  993.5 4.3 fusion.34
  997.8 13.7 %broadcast_select_fusion.3 = bf16[1024,27,128]{2,1,0:T(8,128)(2,1)S(1)} fusion(bf16[1024,27,128]{2,1,0:T(8,128)(2,1)S(1)} %bitcast.389, pred[1024,27]{1,0:T(8,128)(4,1)S(1)} %copy-done.16), kind=kLoop, calls=%fused_computation.27 | loop fusion | flops 3538944 | bytes 14183424 | tf_op jit(solution)/shard_map/jit(_take)/select_n | solution.py:66
  1011.6 4.3 fusion.31
  1016.5 7.0 fusion.300
  1023.5 30.8 %all-gather.4.cloned.1.call-done = bf16[4096,256]{1,0:T(8,128)(2,1)} async-done(((bf16[1024,256]{1,0:T(8,128)(2,1)}), bf16[4096,256]{1,0:T(8,128)(2,1)}) %all-gather.4.cloned.1.call-update) | async-done | bytes 2097168 | tf_op jit(solution)/shard_map/all_gather | solution.py:163
  (336 shorter events, 155.6 us)
Async XLA Ops:
  6.5 387.6 %copy-start = (bf16[8,64,64]{2,1,0:T(8,128)(2,1)S(1)}, bf16[8,64,64]{2,1,0:T(8,128)(2,1)}, u32[]{:S(2)}) copy-start(bf16[8,64,64]{2,1,0:T(8,128)(2,1)} %param.26) | copy-start | bytes 196612
  6.5 29.9 %copy-start.11 = (bf16[4,64,64]{2,1,0:T(8,128)(2,1)S(1)}, bf16[4,64,64]{2,1,0:T(8,128)(2,1)}, u32[]{:S(2)}) copy-start(bf16[4,64,64]{2,1,0:T(8,128)(2,1)} %param.29) | copy-start | bytes 98308
  6.5 25.2 %copy-start.24 = (s32[1024,108]{0,1:T(8,128)S(1)}, s32[1024,108]{0,1:T(8,128)}, u32[]{:S(2)}) copy-start(s32[1024,108]{0,1:T(8,128)} %param.21) | copy-start | bytes 1327108
  6.5 30.7 %copy-start.9 = (bf16[2,64,64]{2,1,0:T(8,128)(2,1)S(1)}, bf16[2,64,64]{2,1,0:T(8,128)(2,1)}, u32[]{:S(2)}) copy-start(bf16[2,64,64]{2,1,0:T(8,128)(2,1)} %param.28) | copy-start | bytes 49156
  6.5 34.3 %copy-start.2 = (bf16[108,64,64]{0,2,1:T(8,128)(2,1)S(1)}, bf16[108,64,64]{0,2,1:T(8,128)(2,1)}, u32[]{:S(2)}) copy-start(bf16[108,64,64]{0,2,1:T(8,128)(2,1)} %param.27) | copy-start | bytes 2654212
  6.5 1047.8 %all-gather.4.cloned.1.call-start = ((), (), s32[]{:S(2)}) async-start(), calls=%async_computation | async-start | bytes 2621440 | tf_op jit(solution)/shard_map/all_gather | solution.py:163
  10.5 379.0 %collective-permute-start.2 = (bf16[768,128]{1,0:T(8,128)(2,1)}, bf16[768,128]{1,0:T(8,128)(2,1)}, u32[]{:S(2)}, u32[]{:S(2)}) collective-permute-start(bf16[768,128]{1,0:T(8,128)(2,1)} %copy.487), channel_id=1, source_target_pairs={{0,4},{4,8},{8,12},{12,16},{16,20},{20,24},{24,28},{28,32},{32,36}... | collective-permute-start | bytes 589832 | tf_op jit(solution)/shard_map/ppermute | solution.py:18
  13.3 376.3 %collective-permute-start.3 = (bf16[768,128]{1,0:T(8,128)(2,1)}, bf16[768,128]{1,0:T(8,128)(2,1)}, u32[]{:S(2)}, u32[]{:S(2)}) collective-permute-start(bf16[768,128]{1,0:T(8,128)(2,1)} %copy.488), channel_id=1, source_target_pairs={{4,0},{8,4},{12,8},{16,12},{20,16},{24,20},{28,24},{32,28},{36,32}... | collective-permute-start | bytes 589832 | tf_op jit(solution)/shard_map/ppermute | solution.py:20
  15.3 89.3 %collective-permute-start = (bf16[2,64,256]{2,1,0:T(8,128)(2,1)}, bf16[2,64,256]{2,1,0:T(8,128)(2,1)}, u32[]{:S(2)}, u32[]{:S(2)}) collective-permute-start(bf16[2,64,256]{2,1,0:T(8,128)(2,1)} %get-tuple-element.6), channel_id=1, source_target_pairs={{0,4},{4,8},{8,12},{12,16},{16,20},{20,24},{24,28},{28,32},{32,36}... | collective-permute-start | bytes 196616 | tf_op jit(solution)/shard_map/ppermute | solution.py:18
  20.1 84.4 %collective-permute-start.1 = (bf16[2,64,256]{2,1,0:T(8,128)(2,1)}, bf16[2,64,256]{2,1,0:T(8,128)(2,1)}, u32[]{:S(2)}, u32[]{:S(2)}) collective-permute-start(bf16[2,64,256]{2,1,0:T(8,128)(2,1)} %get-tuple-element.8), channel_id=1, source_target_pairs={{4,0},{8,4},{12,8},{16,12},{20,16},{24,20},{28,24},{32,28},{36,32}... | collective-permute-start | bytes 196616 | tf_op jit(solution)/shard_map/ppermute | solution.py:20
  64.0 19.5 %copy-start.35 = (s32[128,27]{0,1:T(8,128)S(1)}, s32[128,27]{0,1:T(8,128)}, u32[]{:S(2)}) copy-start(s32[128,27]{0,1:T(8,128)} %get-tuple-element.37) | copy-start | bytes 41476
  64.0 20.4 %copy-start.41 = (pred[128,27]{0,1:T(8,128)(4,1)S(1)}, pred[128,27]{0,1:T(8,128)(4,1)}, u32[]{:S(2)}) copy-start(pred[128,27]{0,1:T(8,128)(4,1)} %get-tuple-element.33) | copy-start | bytes 10372
  64.0 25.9 %copy-start.23 = (s32[1024,27]{0,1:T(8,128)S(1)}, s32[1024,27]{0,1:T(8,128)}, u32[]{:S(2)}) copy-start(s32[1024,27]{0,1:T(8,128)} %get-tuple-element.21) | copy-start | bytes 331780
  64.0 27.3 %copy-start.22 = (s32[1024,27]{0,1:T(8,128)S(1)}, s32[1024,27]{0,1:T(8,128)}, u32[]{:S(2)}) copy-start(s32[1024,27]{0,1:T(8,128)} %get-tuple-element.20) | copy-start | bytes 331780
  67.5 26.1 %copy-start.21 = (s32[1024,27]{0,1:T(8,128)S(1)}, s32[1024,27]{0,1:T(8,128)}, u32[]{:S(2)}) copy-start(s32[1024,27]{0,1:T(8,128)} %get-tuple-element.19) | copy-start | bytes 331780
  73.2 26.3 %copy-start.29 = (s32[1024,9]{0,1:T(8,128)S(1)}, s32[1024,9]{0,1:T(8,128)}, u32[]{:S(2)}) copy-start(s32[1024,9]{0,1:T(8,128)} %get-tuple-element.30) | copy-start | bytes 110596
  77.4 24.3 %copy-start.28 = (s32[1024,9]{0,1:T(8,128)S(1)}, s32[1024,9]{0,1:T(8,128)}, u32[]{:S(2)}) copy-start(s32[1024,9]{0,1:T(8,128)} %get-tuple-element.28) | copy-start | bytes 110596
  256.4 71.8 %copy-start.18 = (pred[1024,9]{1,0:T(8,128)(4,1)S(1)}, pred[1024,9]{1,0:T(8,128)(4,1)}, u32[]{:S(2)}) copy-start(pred[1024,9]{1,0:T(8,128)(4,1)} %copy.482) | copy-start | bytes 27652
  328.2 22.5 %slice-start.3 = ((s8[9437184]{0:T(1024)(128)(4,1)}), s8[4194304]{0:T(1024)(128)(4,1)S(1)}, s32[]{:S(2)}) async-start(s8[9437184]{0:T(1024)(128)(4,1)} %bitcast.384), calls=%async_computation.4 | async-start | bytes 8388608
  328.2 22.5 %slice-start.4 = ((s8[9437184]{0:T(1024)(128)(4,1)}), s8[4194304]{0:T(1024)(128)(4,1)S(1)}, s32[]{:S(2)}) async-start(s8[9437184]{0:T(1024)(128)(4,1)} %bitcast.384), calls=%async_computation.5 | async-start | bytes 8388608
  346.7 20.7 %slice-start = ((s8[9437184]{0:T(1024)(128)(4,1)}), s8[4194304]{0:T(1024)(128)(4,1)S(1)}, s32[]{:S(2)}) async-start(s8[9437184]{0:T(1024)(128)(4,1)} %bitcast.381), calls=%async_computation.1 | async-start | bytes 8388608
  346.7 20.7 %slice-start.1 = ((s8[9437184]{0:T(1024)(128)(4,1)}), s8[1048576]{0:T(1024)(128)(4,1)S(1)}, s32[]{:S(2)}) async-start(s8[9437184]{0:T(1024)(128)(4,1)} %bitcast.381), calls=%async_computation.2 | async-start | bytes 2097152
  389.5 34.2 %copy-start.10 = (bf16[2,64,64]{2,1,0:T(8,128)(2,1)S(1)}, bf16[2,64,64]{2,1,0:T(8,128)(2,1)}, u32[]{:S(2)}) copy-start(bf16[2,64,64]{2,1,0:T(8,128)(2,1)} %param.28) | copy-start | bytes 49156
  389.5 35.2 %copy-start.12 = (bf16[4,64,64]{2,1,0:T(8,128)(2,1)S(1)}, bf16[4,64,64]{2,1,0:T(8,128)(2,1)}, u32[]{:S(2)}) copy-start(bf16[4,64,64]{2,1,0:T(8,128)(2,1)} %param.29) | copy-start | bytes 98308
  389.5 47.4 %copy-start.37 = (s32[1024]{0:T(1024)S(1)}, s32[1024]{0:T(1024)}, u32[]{:S(2)}) copy-start(s32[1024]{0:T(1024)} %pad_clamp_fusion.7) | copy-start | bytes 12292
  389.5 49.0 %copy-start.38 = (s32[1024]{0:T(1024)S(1)}, s32[1024]{0:T(1024)}, u32[]{:S(2)}) copy-start(s32[1024]{0:T(1024)} %pad_clamp_fusion.6) | copy-start | bytes 12292
  389.6 51.2 %copy-start.39 = (s32[1024]{0:T(1024)S(1)}, s32[1024]{0:T(1024)}, u32[]{:S(2)}) copy-start(s32[1024]{0:T(1024)} %pad_clamp_fusion.5) | copy-start | bytes 12292
  394.7 54.3 %copy-start.6 = (bf16[27,128,128]{2,1,0:T(8,128)(2,1)S(1)}, bf16[27,128,128]{2,1,0:T(8,128)(2,1)}, u32[]{:S(2)}) copy-start(bf16[27,128,128]{2,1,0:T(8,128)(2,1)} %reshape.268) | copy-start | bytes 2654212
  973.3 24.5 %slice-start.6 = ((s8[8388608]{0:T(1024)(128)(4,1)}), s8[4194304]{0:T(1024)(128)(4,1)S(1)}, s32[]{:S(2)}) async-start(s8[8388608]{0:T(1024)(128)(4,1)} %bitcast.388), calls=%async_computation.7 | async-start | bytes 8388608
  977.7 20.1 %slice-start.7 = ((s8[8388608]{0:T(1024)(128)(4,1)}), s8[4194304]{0:T(1024)(128)(4,1)S(1)}, s32[]{:S(2)}) async-start(s8[8388608]{0:T(1024)(128)(4,1)} %bitcast.388), calls=%async_computation.8 | async-start | bytes 8388608
  1016.5 40.1 %copy-start.3 = (f32[2,1024,256]{2,1,0:T(8,128)S(1)}, f32[2,1024,256]{2,1,0:T(8,128)}, u32[]{:S(2)}) copy-start(f32[2,1024,256]{2,1,0:T(8,128)} %param.19) | copy-start | bytes 6291460
  1016.5 43.4 %copy-start.1 = (bf16[8,64,64]{2,1,0:T(8,128)(2,1)S(1)}, bf16[8,64,64]{2,1,0:T(8,128)(2,1)}, u32[]{:S(2)}) copy-start(bf16[8,64,64]{2,1,0:T(8,128)(2,1)} %param.26) | copy-start | bytes 196612
  (31 other events, 372.2 us)
Sparse Core Ops, SparseCore 0:
  1023.6 30.6 all-gather.3
